TPU v7x, 1024 devices: a whole 4x8x16 slice. The times are simulated.
1024 devices in a mesh: sub: 32 (over y, z_hi), con: 32 (over x, z_lo, core).
Axes of the slice: x: 4, y: 8, z: 16 (z_hi: 4, z_lo: 4; z = z_hi * 4 + z_lo), core: 2. Of those that a mesh axis runs over, the one named last changes fastest.
Arguments:
- free_velocity: float32 [6, 65536], P(None, 'sub'), may hold values from -6 to 6
- inverse_mass: float32 [6, 65536], P(None, 'sub'), may hold values from 0.25 to 1
- contact_pair: int32 [2, 524288], P(None, ('sub', 'con')), may hold values from 0 to 2047, as said below
- jac_near: float32 [3, 6, 524288], P(None, None, ('sub', 'con')), may hold values from -2.5 to 2.5
- jac_far: float32 [3, 6, 524288], P(None, None, ('sub', 'con')), may hold values from -2.5 to 2.5
- inverse_delassus: float32 [3, 3, 524288], P(None, None, ('sub', 'con')), may hold values from -0.05 to 0.3
- friction: float32 [524288], P(('sub', 'con')), may hold values from 0.3 to 0.9
- velocity_bias: float32 [3, 524288], P(None, ('sub', 'con')), may hold values from -6 to 6
- warm_reaction: float32 [3, 524288], P(None, ('sub', 'con')), may hold values from -2 to 2
- active_flag: int32 [524288], P(('sub', 'con')), may hold values 0 or 1
- sticking_flag: int32 [524288], P(('sub', 'con')), may hold values 0 or 1
- next_list: int32 [32, 256], P('sub'), may hold values from 0 to 2048, as said below
- prev_list: int32 [32, 256], P('sub'), may hold values from 0 to 2048, as said below
Outputs:
- velocity: float32 [6, 65536], P(None, 'sub')
- reaction: float32 [3, 524288], P(None, ('sub', 'con'))
Inputs may be any that keep to these rules, and one draw needn't show every extreme that they name: `contact_pair`: the two bodies of a contact differ. non-empty slots of a row come first and name distinct bodies; slot k of next_list row s is empty exactly when slot k of prev_list row s + 1 is; the last row of next_list and the first row of prev_list are empty; at least half of each other row's slots are filled, and some row has all 256 filled. `prev_list`: see next_list.
All inputs are finite; a program needn't handle non-finite values. No bound on the sum of `active_flag` or of `sticking_flag` on one device may be relied on, other than what follows from the above.
Results may differ from a plain program's by a relative error of at most 0.0001.
Values sent between devices are 32-bit elements; how exact they have to be, the bound alone decides.
A program may use at most 32 MiB of HBM per device.

v0:
```python
import jax
import jax.numpy as jnp
from jax import lax
from jax.sharding import PartitionSpec as P

PASSES = 3


def from_behind(block, axis, distance):
    devices = range(lax.axis_size(axis))
    route = [(i - distance, i) for i in devices if i - distance in devices]
    return lax.ppermute(block, axis, route)


def body(
    free_velocity,
    inverse_mass,
    contact_pair,
    jac_near,
    jac_far,
    inverse_delassus,
    friction,
    velocity_bias,
    warm_reaction,
    active_flag,
    sticking_flag,
    next_list,
    prev_list,
):
    contacts = contact_pair.shape[1]
    both_ends = jnp.concatenate([contact_pair[0], contact_pair[1]])
    next_rows = next_list[0]
    prev_rows = prev_list[0]
    capacity = next_rows.shape[0]
    slots_all = jnp.concatenate([next_rows, prev_rows])
    bodies = free_velocity.shape[1]
    shared = jnp.ones((bodies,), jnp.float32).at[slots_all].add(1.0, mode="drop")
    bound_scale = friction * (1.0 + 0.5 * sticking_flag.astype(jnp.float32))
    live = active_flag.astype(jnp.float32)

    def average(own):
        outgoing = jnp.take(own, slots_all, axis=1, mode="fill", fill_value=0.0)
        to_next = outgoing[:, :capacity]
        to_prev = outgoing[:, capacity:]
        from_before = from_behind(to_next, "sub", 1)
        from_after = from_behind(to_prev, "sub", -1)
        incoming = jnp.concatenate([from_after, from_before], axis=1)
        total = own.at[:, slots_all].add(incoming, mode="drop")
        return total / shared

    def velocity_of(reaction):
        term_near = jnp.sum(jac_near * reaction[:, None, :], axis=0)
        term_far = jnp.sum(jac_far * reaction[:, None, :], axis=0)
        terms = jnp.concatenate([term_near, term_far], axis=1)
        partial_sum = jnp.zeros((6, bodies), jnp.float32).at[:, both_ends].add(terms)
        impulse = lax.psum(partial_sum, "con")
        own = free_velocity + inverse_mass * impulse
        return average(own)

    reaction = warm_reaction
    for step in range(PASSES):
        velocity = velocity_of(reaction)
        ends_vel = jnp.take(velocity, both_ends, axis=1)
        near_vel = ends_vel[:, :contacts]
        far_vel = ends_vel[:, contacts:]
        relative = (
            jnp.sum(jac_near * near_vel[None], axis=1)
            + jnp.sum(jac_far * far_vel[None], axis=1)
            + velocity_bias
        )
        trial = reaction - jnp.sum(inverse_delassus * relative[None, :, :], axis=1)
        normal = jnp.maximum(trial[0], 0.0)
        limit = bound_scale * normal
        tangent = jnp.clip(trial[1:], -limit, limit)
        reaction = jnp.concatenate([normal[None], tangent], axis=0) * live
    velocity = velocity_of(reaction)
    return (velocity, reaction)


def solution(mesh):
    in_specs = (
        P(None, "sub"),
        P(None, "sub"),
        P(None, ("sub", "con")),
        P(None, None, ("sub", "con")),
        P(None, None, ("sub", "con")),
        P(None, None, ("sub", "con")),
        P(("sub", "con")),
        P(None, ("sub", "con")),
        P(None, ("sub", "con")),
        P(("sub", "con")),
        P(("sub", "con")),
        P("sub", None),
        P("sub", None),
    )
    out_specs = (P(None, "sub"), P(None, ("sub", "con")))
    return jax.shard_map(body, mesh=mesh, in_specs=in_specs, out_specs=out_specs, check_vma=False)
```

profile of v0, /device:TPU:40, one launch (start us, length us, event | category | flops | bytes accessed | tf_op | source)
XLA Modules:
  0.0 686.9 jit_solution(1613689234538533180)
XLA Ops:
  0.6 0.7 copy-done.11
  1.4 0.6 copy-done.12
  2.1 0.8 multiply_reduce_fusion.13
  2.9 0.2 copy.76
  3.2 6.3 scatter_custom_fusion
  9.5 0.3 copy.77
  9.8 140.9 %psum.28 = f32[6,2048]{1,0:T(8,128)S(1)} all-reduce(f32[6,2048]{1,0:T(8,128)S(1)} %copy.77), channel_id=1, replica_groups=mesh['sub'=32,'con'=32] {'con'}, use_global_device_ids=true, to_apply=%region_3.0 | all-reduce | flops 12288 | bytes 98304 | tf_op jit(solution)/shard_map/psum | solution.py:56
  150.7 0.4 copy.81
  151.1 1.0 gather_fusion
  152.3 16.4 %collective-permute-start = (f32[6,256]{0,1:T(8,128)S(1)}, f32[6,256]{0,1:T(8,128)S(1)}, u32[]{:S(2)}, u32[]{:S(2)}) collective-permute-start(f32[6,256]{0,1:T(8,128)S(1)} %get-tuple-element.38), channel_id=1, source_target_pairs={{32,0},{64,32},{96,64},{128,96},{160,128},{192,160},{224,192},{256... | collective-permute-start | bytes 18440 | tf_op jit(solution)/shard_map/ppermute | solution.py:12
  168.7 1.9 collective-permute-start.1
  170.7 0.7 copy-done.13
  171.3 3.3 scatter_custom_fusion.2
  174.7 5.6 collective-permute-done.1
  180.6 3.7 scatter_fusion
  184.3 0.3 broadcast_divide_fusion.3
  184.6 2.8 gather_fusion.1
  187.5 0.2 select_bitcast_fusion.2
  187.9 0.7 copy-done
  188.7 0.6 copy-done.5
  189.5 0.6 copy-done.8
  190.3 0.2 copy.85
  190.5 6.3 scatter_custom_fusion.3
  196.8 0.3 copy.86
  197.1 133.4 %psum.29 = f32[6,2048]{1,0:T(8,128)S(1)} all-reduce(f32[6,2048]{1,0:T(8,128)S(1)} %copy.86), channel_id=1, replica_groups=mesh['sub'=32,'con'=32] {'con'}, use_global_device_ids=true, to_apply=%region_12.15 | all-reduce | flops 12288 | bytes 98304 | tf_op jit(solution)/shard_map/psum | solution.py:56
  330.5 0.4 copy.90
  330.9 1.0 gather_fusion.2
  332.1 3.0 collective-permute-start.2
  335.1 6.8 collective-permute-start.3
  341.9 1.0 collective-permute-done.2
  343.0 3.8 collective-permute-done.3
  346.9 0.2 copy.91
  347.0 3.9 scatter_fusion.1
  350.9 0.3 broadcast_divide_fusion.2
  351.3 2.8 gather_fusion.3
  354.1 0.2 select_bitcast_fusion.1
  354.8 0.2 copy.94
  355.0 6.3 scatter_custom_fusion.5
  361.3 0.3 copy.95
  361.7 133.8 %psum.30 = f32[6,2048]{1,0:T(8,128)S(1)} all-reduce(f32[6,2048]{1,0:T(8,128)S(1)} %copy.95), channel_id=1, replica_groups=mesh['sub'=32,'con'=32] {'con'}, use_global_device_ids=true, to_apply=%region_20.23 | all-reduce | flops 12288 | bytes 98304 | tf_op jit(solution)/shard_map/psum | solution.py:56
  495.5 0.4 copy.99
  495.9 1.0 gather_fusion.4
  497.1 2.9 collective-permute-start.4
  500.0 6.8 collective-permute-start.5
  506.8 1.0 collective-permute-done.4
  507.9 5.0 collective-permute-done.5
  513.2 3.7 scatter_fusion.2
  516.9 0.3 broadcast_divide_fusion.1
  517.3 2.8 gather_fusion.5
  520.1 0.2 select_bitcast_fusion
  520.8 0.6 copy-done.7
  521.4 0.2 copy.103
  521.6 6.5 scatter_custom_fusion.7
  528.1 0.3 copy.104
  528.4 133.7 %psum.31 = f32[6,2048]{1,0:T(8,128)S(1)} all-reduce(f32[6,2048]{1,0:T(8,128)S(1)} %copy.104), channel_id=1, replica_groups=mesh['sub'=32,'con'=32] {'con'}, use_global_device_ids=true, to_apply=%region_28.31 | all-reduce | flops 12288 | bytes 98304 | tf_op jit(solution)/shard_map/psum | solution.py:56
  662.2 0.4 copy.108
  662.5 1.0 gather_fusion.6
  663.7 6.3 collective-permute-start.6
  670.0 3.5 collective-permute-start.7
  673.5 1.0 collective-permute-done.6
  674.6 7.1 %collective-permute-done.7 = f32[6,256]{0,1:T(8,128)S(1)} collective-permute-done((f32[6,256]{0,1:T(8,128)S(1)}, f32[6,256]{0,1:T(8,128)S(1)}, u32[]{:S(2)}, u32[]{:S(2)}) %collective-permute-start.7) | collective-permute-done | bytes 6176 | tf_op jit(solution)/shard_map/ppermute | solution.py:12
  681.9 3.7 scatter_fusion.3
  685.6 0.3 broadcast_divide_fusion
  686.0 1.0 copy.110
  (101 shorter events, 3.3 us)
Async XLA Ops:
  0.6 0.7 copy-start.11
  0.6 0.7 copy-start.10
  1.3 0.7 copy-start.12
  1.4 0.7 copy-start.6
  9.8 140.9 %copy-start.2 = (f32[6,2048]{1,0:T(8,128)S(1)}, f32[6,2048]{1,0:T(8,128)}, u32[]{:S(2)}) copy-start(f32[6,2048]{1,0:T(8,128)} %param.17) | copy-start | bytes 147460
  9.8 140.9 %copy-start.3 = (f32[6,2048]{1,0:T(8,128)S(1)}, f32[6,2048]{1,0:T(8,128)}, u32[]{:S(2)}) copy-start(f32[6,2048]{1,0:T(8,128)} %param.18) | copy-start | bytes 147460
  152.3 22.3 %collective-permute-start = (f32[6,256]{0,1:T(8,128)S(1)}, f32[6,256]{0,1:T(8,128)S(1)}, u32[]{:S(2)}, u32[]{:S(2)}) collective-permute-start(f32[6,256]{0,1:T(8,128)S(1)} %get-tuple-element.38), channel_id=1, source_target_pairs={{32,0},{64,32},{96,64},{128,96},{160,128},{192,160},{224,192},{256... | collective-permute-start | bytes 18440 | tf_op jit(solution)/shard_map/ppermute | solution.py:12
  168.7 11.7 %collective-permute-start.1 = (f32[6,256]{0,1:T(8,128)S(1)}, f32[6,256]{0,1:T(8,128)S(1)}, u32[]{:S(2)}, u32[]{:S(2)}) collective-permute-start(f32[6,256]{0,1:T(8,128)S(1)} %get-tuple-element.39), channel_id=1, source_target_pairs={{0,32},{32,64},{64,96},{96,128},{128,160},{160,192},{192,224},{224... | collective-permute-start | bytes 18440 | tf_op jit(solution)/shard_map/ppermute | solution.py:12
  170.6 0.7 copy-start.13
  187.8 0.8 copy-start
  187.8 0.8 copy-start.1
  188.7 0.7 copy-start.5
  188.7 0.7 copy-start.4
  189.5 0.7 copy-start.8
  189.5 0.7 copy-start.9
  332.1 10.8 %collective-permute-start.2 = (f32[6,256]{0,1:T(8,128)S(1)}, f32[6,256]{0,1:T(8,128)S(1)}, u32[]{:S(2)}, u32[]{:S(2)}) collective-permute-start(f32[6,256]{0,1:T(8,128)S(1)} %get-tuple-element.36), channel_id=1, source_target_pairs={{32,0},{64,32},{96,64},{128,96},{160,128},{192,160},{224,192},{256... | collective-permute-start | bytes 18440 | tf_op jit(solution)/shard_map/ppermute | solution.py:12
  335.1 11.7 %collective-permute-start.3 = (f32[6,256]{0,1:T(8,128)S(1)}, f32[6,256]{0,1:T(8,128)S(1)}, u32[]{:S(2)}, u32[]{:S(2)}) collective-permute-start(f32[6,256]{0,1:T(8,128)S(1)} %get-tuple-element.37), channel_id=1, source_target_pairs={{0,32},{32,64},{64,96},{96,128},{128,160},{160,192},{192,224},{224... | collective-permute-start | bytes 18440 | tf_op jit(solution)/shard_map/ppermute | solution.py:12
  497.1 10.8 %collective-permute-start.4 = (f32[6,256]{0,1:T(8,128)S(1)}, f32[6,256]{0,1:T(8,128)S(1)}, u32[]{:S(2)}, u32[]{:S(2)}) collective-permute-start(f32[6,256]{0,1:T(8,128)S(1)} %get-tuple-element.34), channel_id=1, source_target_pairs={{32,0},{64,32},{96,64},{128,96},{160,128},{192,160},{224,192},{256... | collective-permute-start | bytes 18440 | tf_op jit(solution)/shard_map/ppermute | solution.py:12
  500.0 13.0 %collective-permute-start.5 = (f32[6,256]{0,1:T(8,128)S(1)}, f32[6,256]{0,1:T(8,128)S(1)}, u32[]{:S(2)}, u32[]{:S(2)}) collective-permute-start(f32[6,256]{0,1:T(8,128)S(1)} %get-tuple-element.35), channel_id=1, source_target_pairs={{0,32},{32,64},{64,96},{96,128},{128,160},{160,192},{192,224},{224... | collective-permute-start | bytes 18440 | tf_op jit(solution)/shard_map/ppermute | solution.py:12
  520.8 0.6 copy-start.7
  663.7 10.8 %collective-permute-start.6 = (f32[6,256]{0,1:T(8,128)S(1)}, f32[6,256]{0,1:T(8,128)S(1)}, u32[]{:S(2)}, u32[]{:S(2)}) collective-permute-start(f32[6,256]{0,1:T(8,128)S(1)} %get-tuple-element.32), channel_id=1, source_target_pairs={{32,0},{64,32},{96,64},{128,96},{160,128},{192,160},{224,192},{256... | collective-permute-start | bytes 18440 | tf_op jit(solution)/shard_map/ppermute | solution.py:12
  670.0 11.7 %collective-permute-start.7 = (f32[6,256]{0,1:T(8,128)S(1)}, f32[6,256]{0,1:T(8,128)S(1)}, u32[]{:S(2)}, u32[]{:S(2)}) collective-permute-start(f32[6,256]{0,1:T(8,128)S(1)} %get-tuple-element.33), channel_id=1, source_target_pairs={{0,32},{32,64},{64,96},{96,128},{128,160},{160,192},{192,224},{224... | collective-permute-start | bytes 18440 | tf_op jit(solution)/shard_map/ppermute | solution.py:12
where the time goes:
time: 688 us; the launch traced here: 687 us
  blocking collectives  542 us (79%)
  other arithmetic  47.6 us (7%)
  starting transfers between devices  47.6 us (7%)
  waiting for transfers between devices  24.6 us (4%)
  local copies, waits for them, and re-layouts  24 us (3%)
    psum x4, blocking collectives, velocity_of(): impulse = lax.psum(partial_sum, 'con')  542 us
    ppermute x8, starting transfers between devices, from_behind(): return lax.ppermute(block, axis, route)  47.6 us
    scatter-add x4, other arithmetic, velocity_of(): jnp.zeros((6, bodies), jnp.float32).at[:, both_ends].add(terms)  25.3 us
    ppermute x8, waiting for transfers between devices, from_behind(): return lax.ppermute(block, axis, route)  24.6 us
    scatter-add x4, other arithmetic, average(): total = own.at[:, slots_all].add(incoming, mode='drop')  14.9 us
  transfers between devices with their start and end apart: 8, of which 7 were waited for; matrix products, arithmetic and copies ran while one was open for 1% of the time, Pallas kernels for 0%

commit v1 on v0

v1 whole, which is shorter than its diff:
```python
import jax
import jax.numpy as jnp
from jax import lax
from jax.experimental import pallas as pl
from jax.experimental.pallas import tpu as pltpu
from jax.sharding import PartitionSpec as P

PASSES = 3
EVALS = PASSES + 1
N_CON = 32
BODIES = 2048
CONTACTS = 512
ENDS = 2 * CONTACTS
SLOTS = 256
HIGH = 8
LOW = 256
TILES = 16
MESH = pl.DeviceIdType.MESH
F32 = jnp.float32
BF16 = jnp.bfloat16
OFFSETS = sorted(range(1, N_CON), key=lambda k: -min(k, N_CON - k))


def body_owner(tile):
    return (tile // 4) * 8 + 2 + tile % 4


def two_parts(values):
    rest = values - values.astype(BF16).astype(F32)
    return jnp.concatenate([values, rest], axis=0).astype(BF16)


def dot(a, b):
    return lax.dot_general(a, b, (((1,), (0,)), ((), ())), preferred_element_type=F32)


def join(parts):
    return parts[0:8] + parts[8:16]


def kernel(
    fv, im, pair, jn, jf, invd, fric, bias, warm, act, stick, nxt, prv,
    vel_out, react_out,
    jac, mask, oh_low, oh_next, oh_prev, low_oh, next_oh, prev_oh,
    slot_oh, slot_mask, inv_ends, inv_body, own_fv, own_im, react,
    part, rs, acc, ag,
    rs_send, rs_recv, ag_send, body_recv, slot_recv,
):
    sub = lax.axis_index("sub")
    con = lax.axis_index("con")
    subs = lax.axis_size("sub")
    after = lax.rem(sub + 1, subs)
    before = lax.rem(sub + subs - 1, subs)
    x8 = (con // 8) * 8
    z = lax.rem(con // 2, 4)
    core = lax.rem(con, 2)
    my_tile = (con // 8) * 4 + (z - 1) * 2 + core
    owns_body = jnp.logical_and(z >= 1, z <= 2)

    ag[...] = jnp.zeros_like(ag)

    barrier = pltpu.get_barrier_semaphore()
    for k in OFFSETS:
        pl.semaphore_signal(barrier, inc=1, device_id=(sub, lax.rem(con + k, N_CON)), device_id_type=MESH)
    for c in range(2):
        pl.semaphore_signal(barrier, inc=1, device_id=(before, x8 + 6 + c), device_id_type=MESH)
        pl.semaphore_signal(barrier, inc=1, device_id=(after, x8 + c), device_id_type=MESH)

    ends_row = jnp.concatenate([pair[0:1, :], pair[1:2, :]], axis=1)
    ends_f = jnp.broadcast_to(ends_row.astype(F32), (8, ENDS))
    ends_col = ends_f.T[:, 0:1].astype(jnp.int32)
    high_row = ends_row // LOW
    low_row = ends_row - high_row * LOW
    low_col = lax.rem(ends_col, LOW)
    oh_low[...] = (lax.broadcasted_iota(jnp.int32, (ENDS, LOW), 1) == low_col).astype(F32).astype(BF16)
    oh_next[...] = (nxt[...] == ends_col).astype(F32).astype(BF16)
    oh_prev[...] = (prv[...] == ends_col).astype(F32).astype(BF16)
    for h in range(HIGH):
        mask[h * 16:(h + 1) * 16, :] = jnp.broadcast_to((high_row == h).astype(F32), (16, ENDS)).astype(BF16)
    jac[...] = jnp.zeros_like(jac)
    jac[:, 0:6, 0:CONTACTS] = jn[...]
    jac[:, 0:6, CONTACTS:ENDS] = jf[...]
    react[...] = warm[...]

    def make_sums(e):
        reaction = react[...]
        both = jnp.concatenate([reaction, reaction], axis=1)
        terms = jac[0] * both[0:1] + jac[1] * both[1:2] + jac[2] * both[2:3]
        parts = two_parts(terms)
        to_next = join(dot(parts, oh_next[...]))
        to_prev = join(dot(parts, oh_prev[...]))
        for x in range(4):
            for c in range(2):
                part[e, x * 8 + 6 + c] = to_next[:, c * 128:(c + 1) * 128]
                part[e, x * 8 + c] = to_prev[:, c * 128:(c + 1) * 128]
        spread = jnp.concatenate([parts] * HIGH, axis=0) * mask[...]
        sums = dot(spread, oh_low[...])
        for t in range(TILES):
            rows = join(sums[(t // 2) * 16:(t // 2 + 1) * 16])
            part[e, body_owner(t)] = rows[:, (t % 2) * 128:(t % 2 + 1) * 128]

    def sum_copy(e, k):
        to = lax.rem(con + k, N_CON)
        return pltpu.make_async_remote_copy(
            src_ref=part.at[e, to, pl.ds(0, 6)], dst_ref=rs.at[e, k, pl.ds(0, 6)],
            send_sem=rs_send.at[e], recv_sem=rs_recv.at[e], device_id=(sub, to), device_id_type=MESH)

    def body_copy(e, k):
        return pltpu.make_async_remote_copy(
            src_ref=acc.at[e, pl.ds(0, 6)], dst_ref=ag.at[e, my_tile, pl.ds(0, 6)],
            send_sem=ag_send.at[e], recv_sem=body_recv.at[e],
            device_id=(sub, lax.rem(con + k, N_CON)), device_id_type=MESH)

    def slot_copy(e, to_sub, base, q):
        return pltpu.make_async_remote_copy(
            src_ref=acc.at[e, pl.ds(0, 6)], dst_ref=ag.at[e, base + core, pl.ds(0, 6)],
            send_sem=ag_send.at[e], recv_sem=slot_recv.at[e],
            device_id=(to_sub, x8 + q), device_id_type=MESH)

    def all_of(ref, send, recv):
        return pltpu.make_async_remote_copy(
            src_ref=ref, dst_ref=ref, send_sem=send, recv_sem=recv,
            device_id=(sub, lax.rem(con + 1, N_CON)), device_id_type=MESH)

    def send_sums(e):
        for k in OFFSETS:
            sum_copy(e, k).start()

    def exchange(e):
        all_of(rs.at[e, pl.ds(1, N_CON - 1), pl.ds(0, 6)], rs_send.at[e], rs_recv.at[e]).wait_recv()
        impulse = jnp.sum(rs[e, 1:N_CON], axis=0) + part[e, con]
        mine = own_fv[con] + own_im[con] * impulse
        acc[e] = mine

        @pl.when(z == 3)
        def _():
            for q in range(8):
                slot_copy(e, after, 18, q).start()

        @pl.when(z == 0)
        def _():
            for q in range(8):
                slot_copy(e, before, 16, q).start()

        @pl.when(owns_body)
        def _():
            for k in OFFSETS:
                body_copy(e, k).start()
            ag[e, my_tile, 0:6] = mine[0:6]
            all_of(ag.at[e, pl.ds(0, TILES - 1), pl.ds(0, 6)], ag_send.at[e], body_recv.at[e]).wait_recv()

        @pl.when(jnp.logical_not(owns_body))
        def _():
            all_of(ag.at[e, pl.ds(0, TILES), pl.ds(0, 6)], ag_send.at[e], body_recv.at[e]).wait_recv()

    def wait_slots(e):
        all_of(ag.at[e, pl.ds(TILES, 4), pl.ds(0, 6)], ag_send.at[e], slot_recv.at[e]).wait_recv()

    def wide(e, tile):
        return jnp.concatenate([ag[e, tile], ag[e, tile + 1]], axis=1)

    def update(e):
        table = jnp.concatenate([two_parts(wide(e, 2 * h)) for h in range(HIGH)], axis=0)
        got = dot(table, low_oh[...])
        at_ends = jnp.zeros((8, ENDS), F32)
        for h in range(HIGH):
            at_ends = jnp.where(high_row == h, join(got[h * 16:(h + 1) * 16]), at_ends)
        wait_slots(e)
        at_ends = at_ends + join(dot(two_parts(wide(e, 16)), next_oh[...]))
        at_ends = at_ends + join(dot(two_parts(wide(e, 18)), prev_oh[...]))
        at_ends = at_ends * inv_ends[...]
        reaction = react[...]
        relative = []
        for i in range(3):
            moved = jnp.sum(jac[i] * at_ends, axis=0, keepdims=True)
            relative.append(moved[:, 0:CONTACTS] + moved[:, CONTACTS:ENDS] + bias[i:i + 1, :])
        trial = []
        for i in range(3):
            step = invd[i, 0:1, :] * relative[0] + invd[i, 1:2, :] * relative[1] + invd[i, 2:3, :] * relative[2]
            trial.append(reaction[i:i + 1, :] - step)
        live = act[...].astype(F32)
        normal = jnp.maximum(trial[0], 0.0)
        limit = fric[...] * (1.0 + 0.5 * stick[...].astype(F32)) * normal
        react[0:1, :] = normal * live
        react[1:2, :] = jnp.minimum(jnp.maximum(trial[1], -limit), limit) * live
        react[2:3, :] = jnp.minimum(jnp.maximum(trial[2], -limit), limit) * live

    make_sums(0)
    pl.semaphore_wait(barrier, N_CON - 1 + jnp.where(owns_body, 0, 8))
    send_sums(0)

    rows_low = lax.broadcasted_iota(jnp.int32, (LOW, ENDS), 0)
    low_oh[...] = (rows_low == low_row).astype(F32).astype(BF16)
    lists_row = jnp.concatenate([nxt[...], prv[...]], axis=1)
    lists_f = jnp.broadcast_to(lists_row.astype(F32), (8, 2 * SLOTS))
    lists_col = lists_f.T[:, 0:1].astype(jnp.int32)
    next_oh[...] = (lists_col[0:SLOTS] == ends_row).astype(F32).astype(BF16)
    prev_oh[...] = (lists_col[SLOTS:2 * SLOTS] == ends_row).astype(F32).astype(BF16)
    ones = jnp.ones((16, SLOTS), BF16)
    inv_ends[...] = 1.0 / (1.0 + dot(ones, next_oh[...])[0:8] + dot(ones, prev_oh[...])[0:8])
    slot_high = lists_row // LOW
    slot_low = lists_row - slot_high * LOW
    slot_oh[...] = (lax.broadcasted_iota(jnp.int32, (2 * SLOTS, LOW), 1) == lax.rem(lists_col, LOW)).astype(F32).astype(BF16)
    for h in range(HIGH):
        slot_mask[h * 16:(h + 1) * 16, :] = jnp.broadcast_to((slot_high == h).astype(F32), (16, 2 * SLOTS)).astype(BF16)
    counts = dot(slot_mask[...], slot_oh[...])
    for h in range(HIGH):
        inv_body[h] = 1.0 / (1.0 + counts[h * 16:h * 16 + 8])
    low_slot = (lax.broadcasted_iota(jnp.int32, (LOW, 2 * SLOTS), 0) == slot_low).astype(F32).astype(BF16)
    for source, own in ((fv, own_fv), (im, own_im)):
        at_slots = jnp.zeros((8, 2 * SLOTS), F32)
        for h in range(HIGH):
            chunk = jnp.concatenate([source[:, h * LOW:(h + 1) * LOW], jnp.zeros((2, LOW), F32)], axis=0)
            own[body_owner(2 * h)] = chunk[:, 0:128]
            own[body_owner(2 * h + 1)] = chunk[:, 128:256]
            at_slots = jnp.where(slot_high == h, join(dot(two_parts(chunk), low_slot)), at_slots)
        for x in range(4):
            for c in range(2):
                own[x * 8 + 6 + c] = at_slots[:, c * 128:(c + 1) * 128]
                own[x * 8 + c] = at_slots[:, SLOTS + c * 128:SLOTS + (c + 1) * 128]

    def one_pass(e, _):
        exchange(e)
        update(e)
        make_sums(e + 1)
        send_sums(e + 1)
        return 0

    lax.fori_loop(0, PASSES, one_pass, 0)
    react_out[...] = react[...]
    exchange(PASSES)
    wait_slots(PASSES)
    incoming = two_parts(jnp.concatenate([wide(PASSES, 16), wide(PASSES, 18)], axis=1))
    added = dot(jnp.concatenate([incoming] * HIGH, axis=0) * slot_mask[...], slot_oh[...])
    for h in range(HIGH):
        total = (wide(PASSES, 2 * h) + join(added[h * 16:(h + 1) * 16])) * inv_body[h]
        vel_out[:, h * LOW:(h + 1) * LOW] = total[0:6]

    def drain(e, _):
        all_of(rs.at[e, pl.ds(1, N_CON - 1), pl.ds(0, 6)], rs_send.at[e], rs_recv.at[e]).wait_send()

        @pl.when(owns_body)
        def _():
            all_of(rs.at[e, pl.ds(1, N_CON - 1), pl.ds(0, 6)], ag_send.at[e], rs_recv.at[e]).wait_send()

        @pl.when(jnp.logical_not(owns_body))
        def _():
            all_of(rs.at[e, pl.ds(1, 8), pl.ds(0, 6)], ag_send.at[e], rs_recv.at[e]).wait_send()

        return 0

    lax.fori_loop(0, EVALS, drain, 0)


def body(
    free_velocity, inverse_mass, contact_pair, jac_near, jac_far, inverse_delassus, friction,
    velocity_bias, warm_reaction, active_flag, sticking_flag, next_list, prev_list,
):
    vmem = pl.BlockSpec(memory_space=pltpu.VMEM)
    tile = (8, 128)
    return pl.pallas_call(
        kernel,
        out_shape=(
            jax.ShapeDtypeStruct((6, BODIES), F32),
            jax.ShapeDtypeStruct((3, CONTACTS), F32),
        ),
        in_specs=[vmem] * 13,
        out_specs=(vmem, vmem),
        scratch_shapes=[
            pltpu.VMEM((3, 8, ENDS), F32),
            pltpu.VMEM((HIGH * 16, ENDS), BF16),
            pltpu.VMEM((ENDS, LOW), BF16),
            pltpu.VMEM((ENDS, SLOTS), BF16),
            pltpu.VMEM((ENDS, SLOTS), BF16),
            pltpu.VMEM((LOW, ENDS), BF16),
            pltpu.VMEM((SLOTS, ENDS), BF16),
            pltpu.VMEM((SLOTS, ENDS), BF16),
            pltpu.VMEM((2 * SLOTS, LOW), BF16),
            pltpu.VMEM((HIGH * 16, 2 * SLOTS), BF16),
            pltpu.VMEM((8, ENDS), F32),
            pltpu.VMEM((HIGH, 8, LOW), F32),
            pltpu.VMEM((N_CON,) + tile, F32),
            pltpu.VMEM((N_CON,) + tile, F32),
            pltpu.VMEM((3, CONTACTS), F32),
            pltpu.VMEM((EVALS, N_CON) + tile, F32),
            pltpu.VMEM((EVALS, N_CON) + tile, F32),
            pltpu.VMEM((EVALS,) + tile, F32),
            pltpu.VMEM((EVALS, TILES + 4) + tile, F32),
            pltpu.SemaphoreType.DMA((EVALS,)),
            pltpu.SemaphoreType.DMA((EVALS,)),
            pltpu.SemaphoreType.DMA((EVALS,)),
            pltpu.SemaphoreType.DMA((EVALS,)),
            pltpu.SemaphoreType.DMA((EVALS,)),
        ],
        compiler_params=pltpu.CompilerParams(
            collective_id=0, has_side_effects=True, vmem_limit_bytes=32 * 1024 * 1024),
    )(
        free_velocity, inverse_mass, contact_pair, jac_near, jac_far, inverse_delassus,
        friction[None, :], velocity_bias, warm_reaction, active_flag[None, :], sticking_flag[None, :],
        next_list, prev_list,
    )


def solution(mesh):
    in_specs = (
        P(None, "sub"),
        P(None, "sub"),
        P(None, ("sub", "con")),
        P(None, None, ("sub", "con")),
        P(None, None, ("sub", "con")),
        P(None, None, ("sub", "con")),
        P(("sub", "con")),
        P(None, ("sub", "con")),
        P(None, ("sub", "con")),
        P(("sub", "con")),
        P(("sub", "con")),
        P("sub", None),
        P("sub", None),
    )
    out_specs = (P(None, "sub"), P(None, ("sub", "con")))
    return jax.shard_map(body, mesh=mesh, in_specs=in_specs, out_specs=out_specs, check_vma=False)
```

time: 688 us -> 78.6 us (0.11)
  the two profiles are of different devices: /device:TPU:40 before, /device:TPU:1 now
where the time goes in v1:
time: 78.6 us; the launch traced here: 78 us
  Pallas kernels  67.3 us (86%)
  local copies, waits for them, and re-layouts  10 us (13%)
    pallas_call x1, Pallas kernels, body(): pl.pallas_call(kernel, out_shape=(jax.ShapeDtypeStruct((6, BODIES), F32),...  67.3 us
    unnamed x28, local copies, waits for them, and re-layouts  10 us

profile of v1, /device:TPU:1, one launch (start us, length us, event | category | flops | bytes accessed | tf_op | source)
XLA Modules:
  0.0 78.0 jit_solution(12955294816909491064)
XLA Ops:
  0.6 0.0 copy-start.7
  0.6 0.0 copy-start.11
  0.7 0.7 copy-done.7
  1.3 0.0 copy-done.11
  1.3 0.0 copy-start
  1.3 0.8 %copy-done = f32[6,2048]{1,0:T(8,128)S(1)} copy-done((f32[6,2048]{1,0:T(8,128)S(1)}, f32[6,2048]{1,0:T(8,128)}, u32[]{:S(2)}) %copy-start) | copy-done | bytes 49176
  2.2 0.0 copy-start.1
  2.2 0.8 %copy-done.1 = f32[6,2048]{1,0:T(8,128)S(1)} copy-done((f32[6,2048]{1,0:T(8,128)S(1)}, f32[6,2048]{1,0:T(8,128)}, u32[]{:S(2)}) %copy-start.1) | copy-done | bytes 49176
  3.0 0.0 copy-start.2
  3.0 0.8 %copy-done.2 = f32[3,6,512]{2,1,0:T(8,128)S(1)} copy-done((f32[3,6,512]{2,1,0:T(8,128)S(1)}, f32[3,6,512]{2,1,0:T(8,128)}, u32[]{:S(2)}) %copy-start.2) | copy-done | bytes 36888
  3.8 0.0 copy-start.3
  3.8 0.8 %copy-done.3 = f32[3,6,512]{2,1,0:T(8,128)S(1)} copy-done((f32[3,6,512]{2,1,0:T(8,128)S(1)}, f32[3,6,512]{2,1,0:T(8,128)}, u32[]{:S(2)}) %copy-start.3) | copy-done | bytes 36888
  4.6 0.0 copy-start.4
  4.6 0.7 copy-done.4
  5.3 0.0 copy-start.5
  5.3 0.7 copy-done.5
  6.0 0.0 copy-start.6
  6.0 0.7 copy-done.6
  6.7 0.0 copy-start.8
  6.7 0.7 copy-done.8
  7.4 0.0 copy-start.9
  7.4 0.7 copy-done.9
  8.1 0.0 copy-start.10
  8.1 0.7 copy-done.10
  8.8 0.0 copy-start.12
  8.8 0.7 copy-done.12
  9.5 67.3 %shard_map.140 = (f32[6,2048]{1,0:T(8,128)S(1)}, f32[3,512]{1,0:T(4,128)S(1)}) custom-call(f32[6,2048]{1,0:T(8,128)S(1)} %copy-done, f32[6,2048]{1,0:T(8,128)S(1)} %copy-done.1, s32[2,512]{1,0:T(2,128)S(1)} %copy-done.7, f32[3,6,512]{2,1,0:T(8,128)S(1)} %copy-done.2, f32[3,6,512]{2,1,0:T(8,128)S(1)} %copy-done.3, f32[3,3,512]{2,1,0:T(4,128)S(1)} %copy-done.4, ...), custom_call_target="tpu_custom_call" | custom-call | tf_op jit(solution)/shard_map/pallas_call | solution.py:261
  76.8 0.6 copy.17
  77.4 0.6 copy.18
Async XLA Ops:
  0.6 0.7 copy-start.7
  0.6 0.7 copy-start.11
  1.3 0.8 %copy-start = (f32[6,2048]{1,0:T(8,128)S(1)}, f32[6,2048]{1,0:T(8,128)}, u32[]{:S(2)}) copy-start(f32[6,2048]{1,0:T(8,128)} %fv.1) | copy-start | bytes 147460
  2.2 0.8 %copy-start.1 = (f32[6,2048]{1,0:T(8,128)S(1)}, f32[6,2048]{1,0:T(8,128)}, u32[]{:S(2)}) copy-start(f32[6,2048]{1,0:T(8,128)} %im.1) | copy-start | bytes 147460
  3.0 0.8 %copy-start.2 = (f32[3,6,512]{2,1,0:T(8,128)S(1)}, f32[3,6,512]{2,1,0:T(8,128)}, u32[]{:S(2)}) copy-start(f32[3,6,512]{2,1,0:T(8,128)} %jn.1) | copy-start | bytes 110596
  3.8 0.8 %copy-start.3 = (f32[3,6,512]{2,1,0:T(8,128)S(1)}, f32[3,6,512]{2,1,0:T(8,128)}, u32[]{:S(2)}) copy-start(f32[3,6,512]{2,1,0:T(8,128)} %jf.1) | copy-start | bytes 110596
  4.6 0.7 copy-start.4
  5.3 0.7 copy-start.5
  6.0 0.7 copy-start.6
  6.7 0.7 copy-start.8
  7.4 0.7 copy-start.9
  8.1 0.7 copy-start.10
  8.8 0.7 copy-start.12
